TPU v7x, 512 devices: a whole 4x4x16 slice. The times are simulated.
512 devices in a mesh: section: 4 (over y_lo, core), seq: 128 (over z, x, y_hi).
Axes of the slice: x: 4, y: 4 (y_hi: 2, y_lo: 2; y = y_hi * 2 + y_lo), z: 16, core: 2. Of those that a mesh axis runs over, the one named last changes fastest.
Arguments:
- skip_rows: bfloat16 [4, 16384, 2048], P('section', 'seq'), may hold values from -6 to 6
- molecule_kv: bfloat16 [4, 2048, 4096], P('section', 'seq'), may hold values from -139 to 139
- norm_gain: float32 [2048], replicated, may hold values from 0.1 to 1.9
- sink_kv: float32 [2048], replicated, may hold values from -4 to 4
- w_query: bfloat16 [2048, 1024], replicated, may hold values from -0.125 to 0.125
Outputs:
- upsampled: bfloat16 [4, 16384, 1024], P('section', 'seq')
All inputs are finite; a program needn't handle non-finite values.
Results may differ from a plain program's by a relative error of at most 0.014.
The roundings to bfloat16 on the way count: a program that leaves them out, or rounds other values in their place, can miss the bound.
Values may be sent and summed in bfloat16 or wider, within the bound.
No kernel may reach another device: no remote copies, remote signals or barrier semaphores. Data moves between devices by JAX's collectives and lax.ppermute only.
A program may use at most 64 MiB of HBM per device.

v0:
```python
import jax
import jax.numpy as jnp
from jax import lax
from jax.sharding import PartitionSpec as P

NH = 16
HD = 64
SHORT = 4
BACK = 3
HQ = 1024


def passed_along(block, axis, distance):
    devices = range(lax.axis_size(axis))
    route = [((i - distance) % len(devices), i) for i in devices]
    return lax.ppermute(block, axis, route)


def from_behind(value, axis, steps):
    count = lax.axis_size(axis)
    leading, last = (max(0, -steps), min(count, count - steps))
    return lax.ppermute(value, axis, [(source, source + steps) for source in range(leading, last)])


def norm_rows(rows, gain):
    values = rows.astype(jnp.float32)
    inverse = lax.rsqrt(jnp.mean(values * values, axis=-1, keepdims=True) + 1e-06)
    return (values * inverse * gain).astype(jnp.bfloat16)


def attend(query, keyval, sink_kv, block_index, mol_dev):
    chars = query.shape[0]
    width = keyval.shape[1]
    query_heads = query.reshape(chars, NH, HD)
    keys = keyval[:HQ].reshape(NH, HD, width)
    values = keyval[HQ:].reshape(NH, HD, width)
    sink_key = sink_kv[:HQ].reshape(NH, HD)
    sink_value = sink_kv[HQ:].reshape(NH, HD)
    scores = (
        jnp.einsum("qhd,hdk->hqk", query_heads, keys, preferred_element_type=jnp.float32) * 0.125
    )
    sink = jnp.sum(query_heads.astype(jnp.float32) * sink_key[None], axis=-1).T * 0.125
    place = block_index * chars + jnp.arange(chars, dtype=jnp.int32)
    molecule = (block_index - BACK) * mol_dev + jnp.arange(width, dtype=jnp.int32)
    lag = place[:, None] - SHORT * molecule[None, :] - (SHORT - 1)
    visible = (molecule[None, :] >= 0) & (lag >= 0) & (lag < SHORT * BACK * mol_dev)
    scores = jnp.where(visible[None], scores, jnp.float32(-1e30))
    top = jnp.maximum(jnp.max(scores, axis=-1), sink)
    expo = jnp.exp(scores - top[..., None])
    sink_expo = jnp.exp(sink - top)
    total = jnp.sum(expo, axis=-1) + sink_expo
    weight = (expo / total[..., None]).astype(jnp.bfloat16)
    sink_weight = (sink_expo / total).astype(jnp.bfloat16)
    mixed = jnp.einsum("hqk,hdk->qhd", weight, values, preferred_element_type=jnp.float32)
    mixed = mixed + sink_weight.T[..., None].astype(jnp.float32) * sink_value[None]
    return mixed.reshape(chars, HQ).astype(jnp.bfloat16)


def shards(skip_rows, molecule_kv, norm_gain, sink_kv, w_query):
    arrived = passed_along(molecule_kv, "section", 1)
    normed = norm_rows(skip_rows[0], norm_gain)
    query = jnp.dot(normed, w_query, preferred_element_type=jnp.float32).astype(jnp.bfloat16)
    chars = query.shape[0]
    mol_dev = chars // SHORT
    own_block = lax.all_to_all(arrived, "seq", split_axis=2, concat_axis=1, tiled=True)[0]
    pieces = [own_block]
    current = own_block
    for step in range(BACK):
        current = from_behind(current, "seq", 1)
        pieces.insert(0, current)
    keyval = jnp.concatenate(pieces, axis=1)
    block_index = lax.axis_index("seq")
    mixed = attend(query, keyval, sink_kv, block_index, mol_dev)
    return mixed[None]


def solution(mesh):
    return jax.shard_map(
        shards,
        mesh=mesh,
        in_specs=(P("section", "seq", None), P("section", "seq", None), P(), P(), P()),
        out_specs=P("section", "seq", None),
        check_vma=False,
    )
```

profile of v0, /device:TPU:32, one launch (start us, length us, event | category | flops | bytes accessed | tf_op | source)
XLA Modules:
  0.0 130.8 jit_solution(4866062913885767191)
XLA Ops:
  0.0 0.0 copy-start
  0.0 2.0 %collective-permute-start = (bf16[1,16,4096]{2,1,0:T(8,128)(2,1)}, bf16[1,16,4096]{2,1,0:T(8,128)(2,1)S(1)}, u32[]{:S(2)}, u32[]{:S(2)}) collective-permute-start(bf16[1,16,4096]{2,1,0:T(8,128)(2,1)} %param.6), channel_id=1, source_target_pairs={{384,0},{0,128},{128,256},{256,384},{385,1},{1,129},{129,257},{257... | collective-permute-start | bytes 393224 | tf_op jit(solution)/shard_map/ppermute | solution.py:16
  2.1 1.2 fusion.3
  3.3 3.3 %collective-permute-done = bf16[1,16,4096]{2,1,0:T(8,128)(2,1)S(1)} collective-permute-done((bf16[1,16,4096]{2,1,0:T(8,128)(2,1)}, bf16[1,16,4096]{2,1,0:T(8,128)(2,1)S(1)}, u32[]{:S(2)}, u32[]{:S(2)}) %collective-permute-start) | collective-permute-done | bytes 131104 | tf_op jit(solution)/shard_map/ppermute | solution.py:16
  6.6 2.7 %copy.23 = bf16[1,16,4096]{1,0,2:T(2,128)(2,1)S(1)} copy(bf16[1,16,4096]{2,1,0:T(8,128)(2,1)S(1)} %collective-permute-done) | data formatting | bytes 262144 | tf_op jit(solution)/shard_map/ppermute | solution.py:16
  9.3 0.5 broadcast.85
  9.8 22.4 %reduce = bf16[4096,16]{1,0:T(8,128)(2,1)S(1)} reduce(bf16[4096,1,16]{2,1,0:T(2,128)(2,1)S(1)} %bitcast.47, bf16[]{:T(256)} %broadcast.85), dimensions={1}, to_apply=%bitcast.41.reduce_sub_computation | reduce | bytes 262146
  32.2 1.5 %reshape.119 = bf16[128,2,256]{2,1,0:T(2,128)(2,1)} reshape(bf16[4096,16]{1,0:T(8,128)(2,1)S(1)} %reduce) | data formatting | bytes 262144
  33.8 21.6 %all-to-all-start = ((bf16[128,2,256]{2,1,0:T(2,128)(2,1)}), bf16[128,2,256]{2,1,0:T(2,128)(2,1)S(1)}, u32[]{:S(2)}, u32[]{:S(2)}) async-start(bf16[128,2,256]{2,1,0:T(2,128)(2,1)} %reshape.119), calls=%async_computation | async-start | bytes 262144 | tf_op jit(solution)/shard_map/all_to_all | solution.py:65
  55.4 0.0 copy-done
  55.4 3.1 %convolution_convert_fusion = bf16[128,1024]{1,0:T(8,128)(2,1)S(1)} fusion(bf16[2048,1024]{1,0:T(8,128)(2,1)} %param.9, bf16[1,128,2048]{2,1,0:T(8,128)(2,1)} %param.5, f32[2048]{0:T(1024)S(1)} %copy-done, f32[128]{0:T(128)S(1)} %add_rsqrt_fusion), kind=kOutput, calls=%fused_computation.7 | convolution fusion | flops 538050560 | bytes 4989440 | tf_op jit(solution)/shard_map/dot_general | solution.py:62
  58.6 0.0 copy-start.1
  58.6 15.2 %all-to-all-done = bf16[128,2,256]{2,1,0:T(2,128)(2,1)S(1)} async-done(((bf16[128,2,256]{2,1,0:T(2,128)(2,1)}), bf16[128,2,256]{2,1,0:T(2,128)(2,1)S(1)}, u32[]{:S(2)}, u32[]{:S(2)}) %all-to-all-start) | async-done | bytes 131104 | tf_op jit(solution)/shard_map/all_to_all | solution.py:65
  73.8 1.8 %reshape.120 = bf16[4096,1,16]{2,1,0:T(2,128)(2,1)S(1)} reshape(bf16[128,2,256]{2,1,0:T(2,128)(2,1)S(1)} %all-to-all-done) | data formatting | bytes 262144
  75.6 2.0 %copy.24 = bf16[1,16,4096]{2,1,0:T(8,128)(2,1)S(1)} copy(bf16[1,16,4096]{1,0,2:T(2,128)(2,1)S(1)} %bitcast.48) | data formatting | bytes 262144 | tf_op jit(solution)/shard_map/all_to_all | solution.py:65
  77.6 0.4 all_to_all.12
  78.0 0.3 copy.25
  78.3 2.1 %collective-permute-start.1 = (bf16[2048,32]{1,0:T(8,128)(2,1)S(1)}, bf16[2048,32]{1,0:T(8,128)(2,1)S(1)}, u32[]{:S(2)}, u32[]{:S(2)}) collective-permute-start(bf16[2048,32]{1,0:T(8,128)(2,1)S(1)} %bitcast.50), channel_id=1, source_target_pairs={{0,1},{1,2},{2,3},{3,4},{4,5},{5,6},{6,7},{7,8},{8,9},{9,10},{10,1... | collective-permute-start | bytes 393224 | tf_op jit(solution)/shard_map/ppermute | solution.py:22
  80.5 15.4 %collective-permute-done.1 = bf16[2048,32]{1,0:T(8,128)(2,1)S(1)} collective-permute-done((bf16[2048,32]{1,0:T(8,128)(2,1)S(1)}, bf16[2048,32]{1,0:T(8,128)(2,1)S(1)}, u32[]{:S(2)}, u32[]{:S(2)}) %collective-permute-start.1) | collective-permute-done | bytes 131104 | tf_op jit(solution)/shard_map/ppermute | solution.py:22
  95.9 1.9 %collective-permute-start.2 = (bf16[2048,32]{1,0:T(8,128)(2,1)S(1)}, bf16[2048,32]{1,0:T(8,128)(2,1)S(1)}, u32[]{:S(2)}, u32[]{:S(2)}) collective-permute-start(bf16[2048,32]{1,0:T(8,128)(2,1)S(1)} %collective-permute-done.1), channel_id=1, source_target_pairs={{0,1},{1,2},{2,3},{3,4},{4,5},{5,6},{6,7},{7,8},{8,9},{9,10},{10,1... | collective-permute-start | bytes 393224 | tf_op jit(solution)/shard_map/ppermute | solution.py:22
  97.8 0.1 fusion.16
  97.9 14.6 %collective-permute-done.2 = bf16[2048,32]{1,0:T(8,128)(2,1)S(1)} collective-permute-done((bf16[2048,32]{1,0:T(8,128)(2,1)S(1)}, bf16[2048,32]{1,0:T(8,128)(2,1)S(1)}, u32[]{:S(2)}, u32[]{:S(2)}) %collective-permute-start.2) | collective-permute-done | bytes 131104 | tf_op jit(solution)/shard_map/ppermute | solution.py:22
  112.6 1.9 %collective-permute-start.3 = (bf16[2048,32]{1,0:T(8,128)(2,1)S(1)}, bf16[2048,32]{1,0:T(8,128)(2,1)S(1)}, u32[]{:S(2)}, u32[]{:S(2)}) collective-permute-start(bf16[2048,32]{1,0:T(8,128)(2,1)S(1)} %collective-permute-done.2), channel_id=1, source_target_pairs={{0,1},{1,2},{2,3},{3,4},{4,5},{5,6},{6,7},{7,8},{8,9},{9,10},{10,1... | collective-permute-start | bytes 393224 | tf_op jit(solution)/shard_map/ppermute | solution.py:22
  114.5 0.0 copy-done.1
  114.5 0.2 copy.26
  114.7 0.1 mul.88
  114.8 0.1 mul.95
  114.8 0.2 multiply_reduce_fusion
  115.0 13.2 %collective-permute-done.3 = bf16[2048,32]{1,0:T(8,128)(2,1)S(1)} collective-permute-done((bf16[2048,32]{1,0:T(8,128)(2,1)S(1)}, bf16[2048,32]{1,0:T(8,128)(2,1)S(1)}, u32[]{:S(2)}, u32[]{:S(2)}) %collective-permute-start.3) | collective-permute-done | bytes 131104 | tf_op jit(solution)/shard_map/ppermute | solution.py:22
  128.3 0.7 pad_maximum_fusion
  129.0 0.4 fusion.26
  129.4 0.2 fusion.6
  129.6 0.3 fusion.2
  129.9 0.9 copy.28
  (8 shorter events, 0.1 us)
Async XLA Ops:
  0.0 55.4 %copy-start = (f32[2048]{0:T(1024)S(1)}, f32[2048]{0:T(1024)}, u32[]{:S(2)}) copy-start(f32[2048]{0:T(1024)} %param.7) | copy-start | bytes 24580
  0.0 6.6 %collective-permute-start = (bf16[1,16,4096]{2,1,0:T(8,128)(2,1)}, bf16[1,16,4096]{2,1,0:T(8,128)(2,1)S(1)}, u32[]{:S(2)}, u32[]{:S(2)}) collective-permute-start(bf16[1,16,4096]{2,1,0:T(8,128)(2,1)} %param.6), channel_id=1, source_target_pairs={{384,0},{0,128},{128,256},{256,384},{385,1},{1,129},{129,257},{257... | collective-permute-start | bytes 393224 | tf_op jit(solution)/shard_map/ppermute | solution.py:16
  33.8 40.0 %all-to-all-start = ((bf16[128,2,256]{2,1,0:T(2,128)(2,1)}), bf16[128,2,256]{2,1,0:T(2,128)(2,1)S(1)}, u32[]{:S(2)}, u32[]{:S(2)}) async-start(bf16[128,2,256]{2,1,0:T(2,128)(2,1)} %reshape.119), calls=%async_computation | async-start | bytes 262144 | tf_op jit(solution)/shard_map/all_to_all | solution.py:65
  58.6 55.9 %copy-start.1 = (f32[2048]{0:T(1024)S(1)}, f32[2048]{0:T(1024)}, u32[]{:S(2)}) copy-start(f32[2048]{0:T(1024)} %param.8) | copy-start | bytes 24580
  78.3 17.6 %collective-permute-start.1 = (bf16[2048,32]{1,0:T(8,128)(2,1)S(1)}, bf16[2048,32]{1,0:T(8,128)(2,1)S(1)}, u32[]{:S(2)}, u32[]{:S(2)}) collective-permute-start(bf16[2048,32]{1,0:T(8,128)(2,1)S(1)} %bitcast.50), channel_id=1, source_target_pairs={{0,1},{1,2},{2,3},{3,4},{4,5},{5,6},{6,7},{7,8},{8,9},{9,10},{10,1... | collective-permute-start | bytes 393224 | tf_op jit(solution)/shard_map/ppermute | solution.py:22
  95.9 16.6 %collective-permute-start.2 = (bf16[2048,32]{1,0:T(8,128)(2,1)S(1)}, bf16[2048,32]{1,0:T(8,128)(2,1)S(1)}, u32[]{:S(2)}, u32[]{:S(2)}) collective-permute-start(bf16[2048,32]{1,0:T(8,128)(2,1)S(1)} %collective-permute-done.1), channel_id=1, source_target_pairs={{0,1},{1,2},{2,3},{3,4},{4,5},{5,6},{6,7},{7,8},{8,9},{9,10},{10,1... | collective-permute-start | bytes 393224 | tf_op jit(solution)/shard_map/ppermute | solution.py:22
  112.6 15.7 %collective-permute-start.3 = (bf16[2048,32]{1,0:T(8,128)(2,1)S(1)}, bf16[2048,32]{1,0:T(8,128)(2,1)S(1)}, u32[]{:S(2)}, u32[]{:S(2)}) collective-permute-start(bf16[2048,32]{1,0:T(8,128)(2,1)S(1)} %collective-permute-done.2), channel_id=1, source_target_pairs={{0,1},{1,2},{2,3},{3,4},{4,5},{5,6},{6,7},{7,8},{8,9},{9,10},{10,1... | collective-permute-start | bytes 393224 | tf_op jit(solution)/shard_map/ppermute | solution.py:22
where the time goes:
time: 131 us
  waiting for transfers between devices  61.9 us (47%)
  starting transfers between devices  29.6 us (23%)
  other arithmetic  24.9 us (19%)
  local copies, waits for them, and re-layouts  10.4 us (8%)
  matrix products  3.8 us (3%)
    ppermute x3, waiting for transfers between devices, from_behind(): lax.ppermute(value, axis, [(source, source + steps) for source in range(l...  43.3 us
    unnamed x1, other arithmetic  22.4 us
    all_to_all x1, starting transfers between devices, shards(): lax.all_to_all(arrived, 'seq', split_axis=2, concat_axis=1, tiled=True)[0]  21.6 us
    all_to_all x1, waiting for transfers between devices, shards(): lax.all_to_all(arrived, 'seq', split_axis=2, concat_axis=1, tiled=True)[0]  15.2 us
    ppermute x3, starting transfers between devices, from_behind(): lax.ppermute(value, axis, [(source, source + steps) for source in range(l...  5.96 us
    unnamed x7, local copies, waits for them, and re-layouts  3.87 us
    ppermute x1, waiting for transfers between devices, passed_along(): return lax.ppermute(block, axis, route)  3.33 us
    dot_general x1, matrix products, shards(): jnp.dot(normed, w_query, preferred_element_type=jnp.float32)  3.12 us
  transfers between devices with their start and end apart: 5, of which 5 were waited for; matrix products, arithmetic and copies ran while one was open for 4% of the time, Pallas kernels for 0%

commit v1 on v0

--- a/solution.py
+++ b/solution.py
@@ -8,6 +8,12 @@
 SHORT = 4
 BACK = 3
 HQ = 1024
+
+
+def swap_blocks(value, axis, split, join):
+    shards = jnp.split(value, lax.axis_size(axis), axis=split)
+    received = lax.all_to_all(jnp.stack(shards), axis, 0, 0)
+    return jnp.concatenate(received, axis=join)
 
 
 def passed_along(block, axis, distance):
@@ -62,7 +68,7 @@
     query = jnp.dot(normed, w_query, preferred_element_type=jnp.float32).astype(jnp.bfloat16)
     chars = query.shape[0]
     mol_dev = chars // SHORT
-    own_block = lax.all_to_all(arrived, "seq", split_axis=2, concat_axis=1, tiled=True)[0]
+    own_block = swap_blocks(arrived, "seq", 2, 1)[0]
     pieces = [own_block]
     current = own_block
     for step in range(BACK):

time: 131 us -> 109 us (0.83)
  other arithmetic: 24.9 us -> 2.44 us
    unnamed x1 -> x0, other arithmetic: 22.4 us -> none
    unnamed x7 -> x131, local copies, waits for them, and re-layouts: 3.87 us -> 9.23 us
    all_to_all x3 -> x0, local copies, waits for them, and re-layouts: 2.7 us -> none  [shards(): lax.all_to_all(arrived, 'seq', split_axis=2, concat_axis=1, tiled=True)[0]]
    ppermute x1 -> x0, local copies, waits for them, and re-layouts: 2.66 us -> none  [passed_along(): return lax.ppermute(block, axis, route)]
  transfers between devices with their start and end apart: 5 -> 5, of which waited for: 5 -> 5; matrix products, arithmetic and copies ran while one was open for 4% -> 5% of each run, Pallas kernels for 0% -> 0%
where the time goes in v1:
time: 109 us; the launch traced here: 108 us
  waiting for transfers between devices  61.9 us (57%)
  starting transfers between devices  29.6 us (27%)
  local copies, waits for them, and re-layouts  10.5 us (10%)
  matrix products  3.81 us (3%)
  other arithmetic  2.44 us (2%)
    ppermute x3, waiting for transfers between devices, from_behind(): lax.ppermute(value, axis, [(source, source + steps) for source in range(l...  43.3 us
    all_to_all x1, starting transfers between devices, swap_blocks(): received = lax.all_to_all(jnp.stack(shards), axis, 0, 0)  21.6 us
    all_to_all x1, waiting for transfers between devices, swap_blocks(): received = lax.all_to_all(jnp.stack(shards), axis, 0, 0)  15.3 us
    unnamed x131, local copies, waits for them, and re-layouts  9.23 us
    ppermute x3, starting transfers between devices, from_behind(): lax.ppermute(value, axis, [(source, source + steps) for source in range(l...  5.96 us
    ppermute x1, waiting for transfers between devices, passed_along(): return lax.ppermute(block, axis, route)  3.33 us
    dot_general x1, matrix products, shards(): jnp.dot(normed, w_query, preferred_element_type=jnp.float32)  3.13 us
  transfers between devices with their start and end apart: 5, of which 5 were waited for; matrix products, arithmetic and copies ran while one was open for 5% of the time, Pallas kernels for 0%

profile of v1, /device:TPU:32, one launch (start us, length us, event | category | flops | bytes accessed | tf_op | source)
XLA Modules:
  0.0 108.5 jit_solution(9565531094496805174)
XLA Ops:
  0.0 2.0 %collective-permute-start = (bf16[1,16,4096]{2,1,0:T(8,128)(2,1)}, bf16[1,16,4096]{2,1,0:T(8,128)(2,1)S(1)}, u32[]{:S(2)}, u32[]{:S(2)}) collective-permute-start(bf16[1,16,4096]{2,1,0:T(8,128)(2,1)} %param.6), channel_id=1, source_target_pairs={{384,0},{0,128},{128,256},{256,384},{385,1},{1,129},{129,257},{257... | collective-permute-start | bytes 393224 | tf_op jit(solution)/shard_map/ppermute | solution.py:22
  2.1 1.2 %fusion.3 = f32[128]{0:T(128)S(1)} fusion(bf16[1,128,2048]{2,1,0:T(8,128)(2,1)} %param.5), kind=kLoop, calls=%fused_computation.8 | loop fusion | flops 786304 | bytes 524800 | tf_op jit(solution)/shard_map/reduce_sum | solution.py:33
  3.3 3.3 %collective-permute-done = bf16[1,16,4096]{2,1,0:T(8,128)(2,1)S(1)} collective-permute-done((bf16[1,16,4096]{2,1,0:T(8,128)(2,1)}, bf16[1,16,4096]{2,1,0:T(8,128)(2,1)S(1)}, u32[]{:S(2)}, u32[]{:S(2)}) %collective-permute-start) | collective-permute-done | bytes 131104 | tf_op jit(solution)/shard_map/ppermute | solution.py:22
  6.6 0.1 constant_dynamic-update-slice_fusion.126
  7.0 0.1 constant_dynamic-update-slice_fusion.120
  7.2 0.1 constant_dynamic-update-slice_fusion.117
  7.4 0.1 constant_dynamic-update-slice_fusion.114
  7.5 0.1 constant_dynamic-update-slice_fusion.112
  7.7 0.1 constant_dynamic-update-slice_fusion.109
  7.9 0.1 constant_dynamic-update-slice_fusion.106
  8.3 0.1 constant_dynamic-update-slice_fusion.100
  8.8 0.1 constant_dynamic-update-slice_fusion.92
  9.0 0.1 constant_dynamic-update-slice_fusion.89
  9.1 0.1 constant_dynamic-update-slice_fusion.86
  9.5 0.1 constant_dynamic-update-slice_fusion.81
  9.7 0.1 constant_dynamic-update-slice_fusion.78
  10.1 0.1 constant_dynamic-update-slice_fusion.72
  10.2 0.1 constant_dynamic-update-slice_fusion.69
  10.6 0.1 constant_dynamic-update-slice_fusion.64
  10.7 0.1 constant_dynamic-update-slice_fusion.61
  10.9 0.1 constant_dynamic-update-slice_fusion.58
  11.4 0.1 constant_dynamic-update-slice_fusion.50
  11.8 0.1 constant_dynamic-update-slice_fusion.44
  12.0 0.1 constant_dynamic-update-slice_fusion.41
  12.2 0.1 constant_dynamic-update-slice_fusion.38
  12.3 0.1 constant_dynamic-update-slice_fusion.36
  12.5 0.1 constant_dynamic-update-slice_fusion.33
  12.7 0.1 constant_dynamic-update-slice_fusion.30
  13.1 0.1 constant_dynamic-update-slice_fusion.24
  14.7 1.0 reshape.118
  15.7 21.6 %all-to-all-start = ((bf16[128,2,256]{2,1,0:T(2,128)(2,1)}), bf16[128,2,256]{2,1,0:T(2,128)(2,1)S(1)}, u32[]{:S(2)}, u32[]{:S(2)}) async-start(bf16[128,2,256]{2,1,0:T(2,128)(2,1)} %reshape.118), calls=%async_computation | async-start | bytes 262144 | tf_op jit(solution)/shard_map/all_to_all | solution.py:15
  37.4 3.1 %convolution_convert_fusion = bf16[128,1024]{1,0:T(8,128)(2,1)S(1)} fusion(bf16[2048,1024]{1,0:T(8,128)(2,1)} %param.9, bf16[1,128,2048]{2,1,0:T(8,128)(2,1)} %param.5, f32[2048]{0:T(1024)} %param.7, f32[128]{0:T(128)S(1)} %add_rsqrt_fusion), kind=kOutput, calls=%fused_computation.7 | convolution fusion | flops 538050560 | bytes 4989440 | tf_op jit(solution)/shard_map/dot_general | solution.py:68
  40.5 15.3 %all-to-all-done = bf16[128,2,256]{2,1,0:T(2,128)(2,1)S(1)} async-done(((bf16[128,2,256]{2,1,0:T(2,128)(2,1)}), bf16[128,2,256]{2,1,0:T(2,128)(2,1)S(1)}, u32[]{:S(2)}, u32[]{:S(2)}) %all-to-all-start) | async-done | bytes 131104 | tf_op jit(solution)/shard_map/all_to_all | solution.py:15
  55.8 0.3 reshape.119
  56.1 2.1 %collective-permute-start.1 = (bf16[2048,32]{1,0:T(8,128)(2,1)S(1)}, bf16[2048,32]{1,0:T(8,128)(2,1)S(1)}, u32[]{:S(2)}, u32[]{:S(2)}) collective-permute-start(bf16[2048,32]{1,0:T(8,128)(2,1)S(1)} %bitcast.557), channel_id=1, source_target_pairs={{0,1},{1,2},{2,3},{3,4},{4,5},{5,6},{6,7},{7,8},{8,9},{9,10},{10,1... | collective-permute-start | bytes 393224 | tf_op jit(solution)/shard_map/ppermute | solution.py:28
  58.2 15.4 %collective-permute-done.1 = bf16[2048,32]{1,0:T(8,128)(2,1)S(1)} collective-permute-done((bf16[2048,32]{1,0:T(8,128)(2,1)S(1)}, bf16[2048,32]{1,0:T(8,128)(2,1)S(1)}, u32[]{:S(2)}, u32[]{:S(2)}) %collective-permute-start.1) | collective-permute-done | bytes 131104 | tf_op jit(solution)/shard_map/ppermute | solution.py:28
  73.6 1.9 %collective-permute-start.2 = (bf16[2048,32]{1,0:T(8,128)(2,1)S(1)}, bf16[2048,32]{1,0:T(8,128)(2,1)S(1)}, u32[]{:S(2)}, u32[]{:S(2)}) collective-permute-start(bf16[2048,32]{1,0:T(8,128)(2,1)S(1)} %collective-permute-done.1), channel_id=1, source_target_pairs={{0,1},{1,2},{2,3},{3,4},{4,5},{5,6},{6,7},{7,8},{8,9},{9,10},{10,1... | collective-permute-start | bytes 393224 | tf_op jit(solution)/shard_map/ppermute | solution.py:28
  75.5 0.1 fusion.16
  75.7 14.6 %collective-permute-done.2 = bf16[2048,32]{1,0:T(8,128)(2,1)S(1)} collective-permute-done((bf16[2048,32]{1,0:T(8,128)(2,1)S(1)}, bf16[2048,32]{1,0:T(8,128)(2,1)S(1)}, u32[]{:S(2)}, u32[]{:S(2)}) %collective-permute-start.2) | collective-permute-done | bytes 131104 | tf_op jit(solution)/shard_map/ppermute | solution.py:28
  90.3 1.9 %collective-permute-start.3 = (bf16[2048,32]{1,0:T(8,128)(2,1)S(1)}, bf16[2048,32]{1,0:T(8,128)(2,1)S(1)}, u32[]{:S(2)}, u32[]{:S(2)}) collective-permute-start(bf16[2048,32]{1,0:T(8,128)(2,1)S(1)} %collective-permute-done.2), channel_id=1, source_target_pairs={{0,1},{1,2},{2,3},{3,4},{4,5},{5,6},{6,7},{7,8},{8,9},{9,10},{10,1... | collective-permute-start | bytes 393224 | tf_op jit(solution)/shard_map/ppermute | solution.py:28
  92.2 0.2 copy.406
  92.5 0.2 multiply_reduce_fusion
  92.8 13.2 %collective-permute-done.3 = bf16[2048,32]{1,0:T(8,128)(2,1)S(1)} collective-permute-done((bf16[2048,32]{1,0:T(8,128)(2,1)S(1)}, bf16[2048,32]{1,0:T(8,128)(2,1)S(1)}, u32[]{:S(2)}, u32[]{:S(2)}) %collective-permute-start.3) | collective-permute-done | bytes 131104 | tf_op jit(solution)/shard_map/ppermute | solution.py:28
  106.0 0.7 pad_maximum_fusion
  106.7 0.4 fusion.26
  107.1 0.2 fusion.6
  107.3 0.3 fusion.2
  107.6 0.9 copy.408
  (114 shorter events, 6.1 us)
Async XLA Ops:
  0.0 92.2 %copy-start = (f32[2048]{0:T(1024)S(1)}, f32[2048]{0:T(1024)}, u32[]{:S(2)}) copy-start(f32[2048]{0:T(1024)} %param.8) | copy-start | bytes 24580
  0.0 6.6 %collective-permute-start = (bf16[1,16,4096]{2,1,0:T(8,128)(2,1)}, bf16[1,16,4096]{2,1,0:T(8,128)(2,1)S(1)}, u32[]{:S(2)}, u32[]{:S(2)}) collective-permute-start(bf16[1,16,4096]{2,1,0:T(8,128)(2,1)} %param.6), channel_id=1, source_target_pairs={{384,0},{0,128},{128,256},{256,384},{385,1},{1,129},{129,257},{257... | collective-permute-start | bytes 393224 | tf_op jit(solution)/shard_map/ppermute | solution.py:22
  15.7 40.0 %all-to-all-start = ((bf16[128,2,256]{2,1,0:T(2,128)(2,1)}), bf16[128,2,256]{2,1,0:T(2,128)(2,1)S(1)}, u32[]{:S(2)}, u32[]{:S(2)}) async-start(bf16[128,2,256]{2,1,0:T(2,128)(2,1)} %reshape.118), calls=%async_computation | async-start | bytes 262144 | tf_op jit(solution)/shard_map/all_to_all | solution.py:15
  56.1 17.6 %collective-permute-start.1 = (bf16[2048,32]{1,0:T(8,128)(2,1)S(1)}, bf16[2048,32]{1,0:T(8,128)(2,1)S(1)}, u32[]{:S(2)}, u32[]{:S(2)}) collective-permute-start(bf16[2048,32]{1,0:T(8,128)(2,1)S(1)} %bitcast.557), channel_id=1, source_target_pairs={{0,1},{1,2},{2,3},{3,4},{4,5},{5,6},{6,7},{7,8},{8,9},{9,10},{10,1... | collective-permute-start | bytes 393224 | tf_op jit(solution)/shard_map/ppermute | solution.py:28
  73.6 16.6 %collective-permute-start.2 = (bf16[2048,32]{1,0:T(8,128)(2,1)S(1)}, bf16[2048,32]{1,0:T(8,128)(2,1)S(1)}, u32[]{:S(2)}, u32[]{:S(2)}) collective-permute-start(bf16[2048,32]{1,0:T(8,128)(2,1)S(1)} %collective-permute-done.1), channel_id=1, source_target_pairs={{0,1},{1,2},{2,3},{3,4},{4,5},{5,6},{6,7},{7,8},{8,9},{9,10},{10,1... | collective-permute-start | bytes 393224 | tf_op jit(solution)/shard_map/ppermute | solution.py:28
  90.3 15.7 %collective-permute-start.3 = (bf16[2048,32]{1,0:T(8,128)(2,1)S(1)}, bf16[2048,32]{1,0:T(8,128)(2,1)S(1)}, u32[]{:S(2)}, u32[]{:S(2)}) collective-permute-start(bf16[2048,32]{1,0:T(8,128)(2,1)S(1)} %collective-permute-done.2), channel_id=1, source_target_pairs={{0,1},{1,2},{2,3},{3,4},{4,5},{5,6},{6,7},{7,8},{8,9},{9,10},{10,1... | collective-permute-start | bytes 393224 | tf_op jit(solution)/shard_map/ppermute | solution.py:28
